TPU v7x, 32 devices: a whole 2x2x4 slice. The times are simulated.
32 devices in a mesh: ka: 2 (over core), slab: 16 (over z, y, x).
Axes of the slice: x: 2, y: 2, z: 4, core: 2. Of those that a mesh axis runs over, the one named last changes fastest.
Arguments:
- packet_prev: float32 [2, 128, 256, 384], P('ka', 'slab'), may hold values from -18 to 18
- packet_now: float32 [2, 128, 256, 384], P('ka', 'slab'), may hold values from -18 to 18
- potential: float32 [128, 256, 384], P('slab'), may hold values from 0.05 to 0.5
- kin_rho: float32 [128, 128], replicated, may hold values from -1 to 1, as said below
- kin_theta: float32 [256, 256], replicated, may hold values from -1 to 1, as said below
- kin_phi: float32 [384, 384], replicated, may hold values from -1 to 1, as said below
- damping: float32 [128], P('slab'), may hold values from 0.8 to 1
- inertia: float32 [128], P('slab'), may hold values from 0.05 to 0.3
- tilt: float32 [256], replicated, may hold values from 0.5 to 2
Outputs:
- packet_last: float32 [2, 128, 256, 384], P('ka', 'slab')
- packet_before: float32 [2, 128, 256, 384], P('ka', 'slab')
- intersections: float32 [2, 2], P(None, 'ka')
Inputs may be any that keep to these rules, and one draw needn't show every extreme that they name: `kin_rho`: symmetric. `kin_theta`: symmetric. `kin_phi`: symmetric.
All inputs are finite; a program needn't handle non-finite values.
Results may differ from a plain program's by a relative error of at most 0.0001.
Values sent between devices are 32-bit elements; how exact they have to be, the bound alone decides.
A program may use at most 128 MiB of HBM per device.

v0:
```python
import jax
import jax.numpy as jnp
from jax import lax
from jax.sharding import PartitionSpec as P

NR = 128
NT = 256
NP = 384
STEPS = 2
JTOT = 60
K_FIRST = 0
HI = lax.Precision.HIGHEST


def padded(cells, sides, width):
    for axis, dim in sides:
        count = lax.axis_size(axis)
        ends = count - 1
        head = lax.slice_in_dim(cells, 0, width, axis=dim)
        tail = lax.slice_in_dim(cells, cells.shape[dim] - width, cells.shape[dim], axis=dim)
        cells = jnp.concatenate(
            [
                lax.ppermute(tail, axis, [(i, (i + 1) % count) for i in range(ends)]),
                cells,
                lax.ppermute(head, axis, [((i + 1) % count, i) for i in range(ends)]),
            ],
            axis=dim,
        )
    return cells


def rho_apply(kin_rho, whole):
    return jnp.einsum("sr,rtp->stp", kin_rho, whole, precision=HI)


def apply_h(q, potential, kin_rho, kin_theta, kin_phi, inertia, tilt):
    kval = (K_FIRST + lax.axis_index("ka")).astype(jnp.float32)
    jj = float(JTOT * (JTOT + 1))
    cent = (jj - 2.0 * kval * kval) / float(JTOT * JTOT)
    lam_here = jnp.sqrt(jj - kval * (kval + 1.0)) / float(JTOT)
    lam_below = jnp.sqrt(jj - (kval - 1.0) * kval) / float(JTOT)
    near = padded(q, (("ka", 0),), 1)
    field = q[0]
    term = rho_apply(
        kin_rho, lax.all_to_all(field, "slab", split_axis=1, concat_axis=0, tiled=True)
    )
    rho_part = lax.all_to_all(term, "slab", split_axis=0, concat_axis=1, tiled=True)
    theta_part = jnp.einsum("ts,rsp->rtp", kin_theta, field, precision=HI)
    rows = field.shape[0] * field.shape[1]
    phi_part = jnp.dot(field.reshape(rows, field.shape[2]), kin_phi, precision=HI).reshape(
        field.shape
    )
    coupling = (
        inertia[:, None, None] * tilt[None, :, None] * (lam_here * near[2] + lam_below * near[0])
    )
    diag = potential + inertia[:, None, None] * cent
    total = rho_part + theta_part + phi_part + diag * field + coupling
    return total[None]


def shards(packet_prev, packet_now, potential, kin_rho, kin_theta, kin_phi, damping, inertia, tilt):
    damp = damping[None, :, None, None]
    cells = float(NR * NT * NP)
    q_prev = packet_prev
    q = packet_now
    partials = []
    for step in range(STEPS):
        image = apply_h(q, potential, kin_rho, kin_theta, kin_phi, inertia, tilt)
        q_new = damp * (2.0 * image - damp * q_prev)
        local_sum = jnp.sum(packet_now * q_new, axis=(1, 2, 3))
        partials.append(lax.psum(local_sum, "slab") / cells)
        q_prev = q
        q = q_new
    intersections = jnp.stack(partials, axis=0)
    return (q, q_prev, intersections)


def solution(mesh):
    return jax.shard_map(
        shards,
        mesh=mesh,
        in_specs=(
            P("ka", "slab", None, None),
            P("ka", "slab", None, None),
            P("slab", None, None),
            P(),
            P(),
            P(),
            P("slab"),
            P("slab"),
            P(),
        ),
        out_specs=(P("ka", "slab", None, None), P("ka", "slab", None, None), P(None, "ka")),
        check_vma=False,
    )
```

profile of v0, /device:TPU:0, one launch (start us, length us, event | category | flops | bytes accessed | tf_op | source)
XLA Modules:
  0.0 420.4 jit_solution(10612199767086044564)
XLA Ops:
  0.6 3.8 copy.81
  4.4 79.6 %all_to_all.72 = f32[8,256,384]{2,0,1:T(8,128)S(1)} all-to-all(f32[8,256,384]{2,0,1:T(8,128)S(1)} %copy.81), channel_id=1, replica_groups=mesh['ka'=2,'slab'=16] {'slab'}, dimensions={1} | all-to-all | bytes 6291456 | tf_op jit(solution)/shard_map/all_to_all | solution.py:45
  84.0 2.9 fusion.10
  86.9 3.5 copy.84
  90.4 4.5 %all-to-all-start.1 = ((f32[128,16,384]{2,1,0:T(8,128)}), f32[128,16,384]{2,1,0:T(8,128)}, u32[]{:S(2)}, u32[]{:S(2)}) async-start(f32[128,16,384]{2,1,0:T(8,128)} %copy.84), calls=%async_computation.1 | async-start | bytes 6291456 | tf_op jit(solution)/shard_map/all_to_all | solution.py:47
  94.9 3.5 copy.80
  98.5 1.3 collective-permute-start
  99.7 6.4 %collective-permute-start.1 = (f32[1,8,256,384]{2,3,1,0:T(8,128)}, f32[1,8,256,384]{2,3,1,0:T(8,128)}, u32[]{:S(2)}, u32[]{:S(2)}) collective-permute-start(f32[1,8,256,384]{2,3,1,0:T(8,128)} %copy.80), channel_id=1, source_target_pairs={{0,16},{1,17},{2,18},{3,19},{4,20},{5,21},{6,22},{7,23},{8,24},{9,... | collective-permute-start | bytes 9437192 | tf_op jit(solution)/shard_map/ppermute | solution.py:23
  106.2 3.5 copy.89
  109.8 3.6 copy.92
  113.4 8.6 %fusion.22 = f32[8,384,256]{2,1,0:T(8,128)} fusion(f32[256,256]{1,0:T(8,128)S(1)} %copy-done.1, f32[1,8,256,384]{3,2,1,0:T(8,128)} %param.10), kind=kOutput, calls=%fused_computation.29 | convolution fusion | flops 2415919104 | bytes 6553600 | tf_op jit(solution)/shard_map/ts,rsp->rtp/dot_general | solution.py:48
  122.0 33.1 %all-to-all-done.1 = f32[128,16,384]{2,1,0:T(8,128)} async-done(((f32[128,16,384]{2,1,0:T(8,128)}), f32[128,16,384]{2,1,0:T(8,128)}, u32[]{:S(2)}, u32[]{:S(2)}) %all-to-all-start.1) | async-done | bytes 3145760 | tf_op jit(solution)/shard_map/all_to_all | solution.py:47
  155.1 3.9 copy.85
  158.9 3.6 copy.86
  162.5 16.2 %fusion.5 = f32[1,8,256,384]{2,3,1,0:T(8,128)} fusion(f32[8,256,384]{1,2,0:T(8,128)} %copy.86, f32[8,384,256]{2,1,0:T(8,128)} %fusion.22, f32[1,8,256,384]{2,3,1,0:T(8,128)} %copy.80, f32[1,8,256,384]{2,3,1,0:T(8,128)} %copy.92, f32[1,8,256,384]{2,3,1,0:T(8,128)} %collective-permute-done.1, f32[1,8,256,384]{2,3,1,0:T(8,128)} %collective-permute-done, ...), kind=kOutput, calls=%fused_computation.9 | convolution fusion | flops 3634888704 | bytes 28909640 | tf_op jit(solution)/shard_map/dot_general | solution.py:50
  178.7 3.6 copy.93
  182.3 84.8 %all_to_all.73 = f32[8,256,384]{2,0,1:T(8,128)S(1)} all-to-all(f32[8,256,384]{2,0,1:T(8,128)} %copy.93), channel_id=1, replica_groups=mesh['ka'=2,'slab'=16] {'slab'}, dimensions={1} | all-to-all | bytes 6291456 | tf_op jit(solution)/shard_map/all_to_all | solution.py:45
  267.0 0.5 copy.95
  267.6 7.1 %fusion.15 = f32[128,16,384]{0,2,1:T(8,128)} fusion(f32[128,16,384]{2,1,0:T(8,128)S(1)} %bitcast.104, f32[128,128]{1,0:T(8,128)S(1)} %copy-done.2), kind=kOutput, calls=%fused_computation.24 | convolution fusion | flops 1207959552 | bytes 6356992 | tf_op jit(solution)/shard_map/sr,rtp->stp/dot_general | solution.py:33
  274.7 3.7 copy.97
  278.4 4.5 %all-to-all-start.3 = ((f32[128,16,384]{2,1,0:T(8,128)}), f32[128,16,384]{2,1,0:T(8,128)}, u32[]{:S(2)}, u32[]{:S(2)}) async-start(f32[128,16,384]{2,1,0:T(8,128)} %copy.97), calls=%async_computation.3 | async-start | bytes 6291456 | tf_op jit(solution)/shard_map/all_to_all | solution.py:47
  282.9 1.3 collective-permute-start.2
  284.2 6.4 %collective-permute-start.3 = (f32[1,8,256,384]{2,3,1,0:T(8,128)}, f32[1,8,256,384]{2,3,1,0:T(8,128)}, u32[]{:S(2)}, u32[]{:S(2)}) collective-permute-start(f32[1,8,256,384]{2,3,1,0:T(8,128)} %fusion.5), channel_id=1, source_target_pairs={{0,16},{1,17},{2,18},{3,19},{4,20},{5,21},{6,22},{7,23},{8,24},{9,... | collective-permute-start | bytes 9437192 | tf_op jit(solution)/shard_map/ppermute | solution.py:23
  290.6 3.5 copy.106
  294.1 6.2 %fusion.20 = f32[8,384,256]{2,1,0:T(8,128)} fusion(f32[256,256]{1,0:T(8,128)S(1)} %copy-done.1, f32[1,8,256,384]{2,3,1,0:T(8,128)} %fusion.5), kind=kOutput, calls=%fused_computation.27 | convolution fusion | flops 2415919104 | bytes 6553600 | tf_op jit(solution)/shard_map/ts,rsp->rtp/dot_general | solution.py:48
  300.3 42.7 %all-to-all-done.3 = f32[128,16,384]{2,1,0:T(8,128)} async-done(((f32[128,16,384]{2,1,0:T(8,128)}), f32[128,16,384]{2,1,0:T(8,128)}, u32[]{:S(2)}, u32[]{:S(2)}) %all-to-all-start.3) | async-done | bytes 3145760 | tf_op jit(solution)/shard_map/all_to_all | solution.py:47
  343.0 3.9 copy.98
  346.9 3.5 copy.99
  350.4 15.0 %multiply_reduce_fusion.1 = (f32[]{:T(128)}, f32[]{:T(128)}, f32[1,8,256,384]{2,3,1,0:T(8,128)}) fusion(f32[1,8,256,384]{2,3,1,0:T(8,128)} %copy.80, f32[1,8,256,384]{2,3,1,0:T(8,128)} %fusion.5, f32[1,8,256,384]{2,3,1,0:T(8,128)} %collective-permute-done.3, f32[]{:T(128)S(6)} %div.20, f32[1,8,256,384]{2,3,1,0:T(8,128)} %collective-permute-done.2, ...), kind=kOutput, calls=%fused_computation.23 | convolution fusion | flops 3638034432 | bytes 25763920 | tf_op jit(solution)/shard_map/dot_general | solution.py:50
  365.4 49.6 %all-reduce = (f32[1]{0:T(128)}, f32[1]{0:T(128)}) all-reduce(f32[1]{0:T(128)} %bitcast.30, f32[1]{0:T(128)} %bitcast.28), channel_id=1, replica_groups=mesh['ka'=2,'slab'=16] {'slab'}, use_global_device_ids=true, to_apply=%region_3.0 | all-reduce | flops 2 | bytes 16 | tf_op jit(solution)/shard_map/psum | solution.py:71
  416.3 3.5 copy.105
  419.9 0.6 pad_maximum_fusion
  (18 shorter events, 0.1 us)
Async XLA Ops:
  0.6 161.9 %copy-start = (f32[384,384]{1,0:T(8,128)S(1)}, f32[384,384]{1,0:T(8,128)}, u32[]{:S(2)}) copy-start(f32[384,384]{1,0:T(8,128)} %param.14) | copy-start | bytes 1769476
  4.4 79.6 %copy-start.2 = (f32[128,128]{1,0:T(8,128)S(1)}, f32[128,128]{1,0:T(8,128)}, u32[]{:S(2)}) copy-start(f32[128,128]{1,0:T(8,128)} %param.12) | copy-start | bytes 196612
  90.4 64.7 %all-to-all-start.1 = ((f32[128,16,384]{2,1,0:T(8,128)}), f32[128,16,384]{2,1,0:T(8,128)}, u32[]{:S(2)}, u32[]{:S(2)}) async-start(f32[128,16,384]{2,1,0:T(8,128)} %copy.84), calls=%async_computation.1 | async-start | bytes 6291456 | tf_op jit(solution)/shard_map/all_to_all | solution.py:47
  98.5 64.1 %collective-permute-start = (f32[1,8,256,384]{2,3,1,0:T(8,128)}, f32[1,8,256,384]{2,3,1,0:T(8,128)}, u32[]{:S(2)}, u32[]{:S(2)}) collective-permute-start(f32[1,8,256,384]{2,3,1,0:T(8,128)} %copy.80), channel_id=1, source_target_pairs={{16,0},{17,1},{18,2},{19,3},{20,4},{21,5},{22,6},{23,7},{24,8},{25... | collective-permute-start | bytes 9437192 | tf_op jit(solution)/shard_map/ppermute | solution.py:25
  99.7 62.8 %collective-permute-start.1 = (f32[1,8,256,384]{2,3,1,0:T(8,128)}, f32[1,8,256,384]{2,3,1,0:T(8,128)}, u32[]{:S(2)}, u32[]{:S(2)}) collective-permute-start(f32[1,8,256,384]{2,3,1,0:T(8,128)} %copy.80), channel_id=1, source_target_pairs={{0,16},{1,17},{2,18},{3,19},{4,20},{5,21},{6,22},{7,23},{8,24},{9,... | collective-permute-start | bytes 9437192 | tf_op jit(solution)/shard_map/ppermute | solution.py:23
  109.8 3.6 copy-start.5
  109.8 3.6 copy-start.4
  109.8 3.7 copy-start.1
  158.9 3.6 copy-start.3
  278.4 64.6 %all-to-all-start.3 = ((f32[128,16,384]{2,1,0:T(8,128)}), f32[128,16,384]{2,1,0:T(8,128)}, u32[]{:S(2)}, u32[]{:S(2)}) async-start(f32[128,16,384]{2,1,0:T(8,128)} %copy.97), calls=%async_computation.3 | async-start | bytes 6291456 | tf_op jit(solution)/shard_map/all_to_all | solution.py:47
  282.9 67.5 %collective-permute-start.2 = (f32[1,8,256,384]{2,3,1,0:T(8,128)}, f32[1,8,256,384]{2,3,1,0:T(8,128)}, u32[]{:S(2)}, u32[]{:S(2)}) collective-permute-start(f32[1,8,256,384]{2,3,1,0:T(8,128)} %fusion.5), channel_id=1, source_target_pairs={{16,0},{17,1},{18,2},{19,3},{20,4},{21,5},{22,6},{23,7},{24,8},{25... | collective-permute-start | bytes 9437192 | tf_op jit(solution)/shard_map/ppermute | solution.py:25
  284.2 66.2 %collective-permute-start.3 = (f32[1,8,256,384]{2,3,1,0:T(8,128)}, f32[1,8,256,384]{2,3,1,0:T(8,128)}, u32[]{:S(2)}, u32[]{:S(2)}) collective-permute-start(f32[1,8,256,384]{2,3,1,0:T(8,128)} %fusion.5), channel_id=1, source_target_pairs={{0,16},{1,17},{2,18},{3,19},{4,20},{5,21},{6,22},{7,23},{8,24},{9,... | collective-permute-start | bytes 9437192 | tf_op jit(solution)/shard_map/ppermute | solution.py:23
where the time goes:
time: 421 us; the launch traced here: 420 us
  blocking collectives  214 us (51%)
  waiting for transfers between devices  75.8 us (18%)
  matrix products  56 us (13%)
  local copies, waits for them, and re-layouts  47.6 us (11%)
  starting transfers between devices  24.3 us (6%)
    all_to_all x2, blocking collectives, apply_h(): lax.all_to_all(field, 'slab', split_axis=1, concat_axis=0, tiled=True)  164 us
    all_to_all x2, waiting for transfers between devices, apply_h(): lax.all_to_all(term, 'slab', split_axis=0, concat_axis=1, tiled=True)  75.8 us
    psum x1, blocking collectives, shards(): partials.append(lax.psum(local_sum, 'slab') / cells)  49.6 us
    dot_general x2, matrix products, apply_h(): jnp.dot(field.reshape(rows, field.shape[2]), kin_phi, precision=HI)  31.2 us
    unnamed x17, local copies, waits for them, and re-layouts  17.8 us
    all_to_all x4, local copies, waits for them, and re-layouts, apply_h(): lax.all_to_all(term, 'slab', split_axis=0, concat_axis=1, tiled=True)  14.8 us
    dot_general x2, matrix products, apply_h(): theta_part = jnp.einsum('ts,rsp->rtp', kin_theta, field, precision=HI)  14.8 us
    ppermute x2, starting transfers between devices, padded(): lax.ppermute(tail, axis, [(i, (i + 1) % count) for i in range(ends)])  12.8 us
  transfers between devices with their start and end apart: 6, of which 2 were waited for; matrix products, arithmetic and copies ran while one was open for 10% of the time, Pallas kernels for 0%

commit v1 on v0

--- a/solution.py
+++ b/solution.py
@@ -1,3 +1,4 @@
+import functools
 import jax
 import jax.numpy as jnp
 from jax import lax
@@ -10,6 +11,17 @@
 JTOT = 60
 K_FIRST = 0
 HI = lax.Precision.HIGHEST
+
+
+def pipes_press(inputs, axis_tag):
+    e_next = lax.axis_size(axis_tag)
+    local_now = jnp.split(inputs, e_next, axis=1)
+    t1 = jnp.stack(local_now)
+    val = lax.all_to_all(t1, axis_tag, 0, 0)
+    return jnp.concatenate(val, axis=0)
+
+
+_handle_scenes = functools.partial(pipes_press, axis_tag="slab")
 
 
 def padded(cells, sides, width):
@@ -41,9 +53,7 @@
     lam_below = jnp.sqrt(jj - (kval - 1.0) * kval) / float(JTOT)
     near = padded(q, (("ka", 0),), 1)
     field = q[0]
-    term = rho_apply(
-        kin_rho, lax.all_to_all(field, "slab", split_axis=1, concat_axis=0, tiled=True)
-    )
+    term = rho_apply(kin_rho, _handle_scenes(field))
     rho_part = lax.all_to_all(term, "slab", split_axis=0, concat_axis=1, tiled=True)
     theta_part = jnp.einsum("ts,rsp->rtp", kin_theta, field, precision=HI)
     rows = field.shape[0] * field.shape[1]

time: 421 us -> 407 us (0.967)
  local copies, waits for them, and re-layouts: 47.6 us -> 24.3 us
  waiting for transfers between devices: 75.8 us -> 91.7 us
  matrix products: 56 us -> 49.3 us
    all_to_all x2, waiting for transfers between devices: 75.8 us -> 91.7 us  [apply_h(): lax.all_to_all(term, 'slab', split_axis=0, concat_axis=1, tiled=True)]
    all_to_all x4 -> x2, local copies, waits for them, and re-layouts: 14.8 us -> 4.67 us  [apply_h(): lax.all_to_all(term, 'slab', split_axis=0, concat_axis=1, tiled=True)]
    dot_general x2, matrix products: 31.2 us -> 22 us  [apply_h(): jnp.dot(field.reshape(rows, field.shape[2]), kin_phi, precision=HI)]
    squeeze x2 -> x0, local copies, waits for them, and re-layouts: 7.36 us -> none  [apply_h(): field = q[0]]
    unnamed x17 -> x54, local copies, waits for them, and re-layouts: 17.8 us -> 12.3 us
  transfers between devices with their start and end apart: 6 -> 6, of which waited for: 2 -> 2; matrix products, arithmetic and copies ran while one was open for 10% -> 4% of each run, Pallas kernels for 0% -> 0%
where the time goes in v1:
time: 407 us; the launch traced here: 406 us
  blocking collectives  214 us (53%)
  waiting for transfers between devices  91.7 us (23%)
  matrix products  49.3 us (12%)
  starting transfers between devices  24.4 us (6%)
  local copies, waits for them, and re-layouts  24.3 us (6%)
    all_to_all x2, blocking collectives, pipes_press(): val = lax.all_to_all(t1, axis_tag, 0, 0)  164 us
    all_to_all x2, waiting for transfers between devices, apply_h(): lax.all_to_all(term, 'slab', split_axis=0, concat_axis=1, tiled=True)  91.7 us
    psum x1, blocking collectives, shards(): partials.append(lax.psum(local_sum, 'slab') / cells)  49.6 us
    dot_general x2, matrix products, apply_h(): jnp.dot(field.reshape(rows, field.shape[2]), kin_phi, precision=HI)  22 us
    dot_general x2, matrix products, rho_apply(): return jnp.einsum('sr,rtp->stp', kin_rho, whole, precision=HI)  14.2 us
    dot_general x2, matrix products, apply_h(): theta_part = jnp.einsum('ts,rsp->rtp', kin_theta, field, precision=HI)  13 us
    ppermute x2, starting transfers between devices, padded(): lax.ppermute(tail, axis, [(i, (i + 1) % count) for i in range(ends)])  12.7 us
    unnamed x54, local copies, waits for them, and re-layouts  12.3 us
  transfers between devices with their start and end apart: 6, of which 2 were waited for; matrix products, arithmetic and copies ran while one was open for 4% of the time, Pallas kernels for 0%

profile of v1, /device:TPU:0, one launch (start us, length us, event | category | flops | bytes accessed | tf_op | source)
XLA Modules:
  0.0 406.4 jit_solution(14143545182470662240)
XLA Ops:
  0.7 1.1 fusion.57
  1.8 1.0 fusion.56
  2.8 0.9 fusion.55
  3.7 0.9 fusion.54
  4.7 0.9 fusion.53
  5.6 0.9 fusion.52
  6.6 0.9 fusion.51
  7.5 0.9 fusion.50
  8.7 79.6 %all_to_all.46 = f32[16,8,16,384]{3,2,1,0:T(8,128)S(1)} all-to-all(f32[16,8,16,384]{3,2,1,0:T(8,128)S(1)} %fusion.42), channel_id=1, replica_groups=mesh['ka'=2,'slab'=16] {'slab'}, dimensions={0} | all-to-all | bytes 6291456 | tf_op jit(solution)/shard_map/all_to_all | solution.py:20
  88.2 7.1 %fusion.14 = f32[128,16,384]{0,2,1:T(8,128)} fusion(f32[128,16,384]{2,1,0:T(8,128)S(1)} %bitcast.249, f32[128,128]{1,0:T(8,128)S(1)} %copy-done.8), kind=kOutput, calls=%fused_computation.22 | convolution fusion | flops 1207959552 | bytes 6356992 | tf_op jit(solution)/shard_map/sr,rtp->stp/dot_general | solution.py:45
  95.4 3.6 copy.27
  98.9 4.6 %all-to-all-start.1 = ((f32[128,16,384]{2,1,0:T(8,128)}), f32[128,16,384]{2,1,0:T(8,128)}, u32[]{:S(2)}, u32[]{:S(2)}) async-start(f32[128,16,384]{2,1,0:T(8,128)} %copy.27), calls=%async_computation.1 | async-start | bytes 6291456 | tf_op jit(solution)/shard_map/all_to_all | solution.py:57
  103.6 1.3 collective-permute-start
  104.9 6.4 %collective-permute-start.1 = (f32[1,8,256,384]{3,2,1,0:T(8,128)}, f32[1,8,256,384]{3,2,1,0:T(8,128)}, u32[]{:S(2)}, u32[]{:S(2)}) collective-permute-start(f32[1,8,256,384]{3,2,1,0:T(8,128)} %param.10), channel_id=1, source_target_pairs={{0,16},{1,17},{2,18},{3,19},{4,20},{5,21},{6,22},{7,23},{8,24},{9,... | collective-permute-start | bytes 9437192 | tf_op jit(solution)/shard_map/ppermute | solution.py:35
  111.5 6.5 %fusion.24 = f32[8,384,256]{1,2,0:T(8,128)} fusion(f32[256,256]{1,0:T(8,128)S(1)} %copy-done.7, f32[1,8,256,384]{3,2,1,0:T(8,128)} %param.10), kind=kOutput, calls=%fused_computation.28 | convolution fusion | flops 2415919104 | bytes 6553600 | tf_op jit(solution)/shard_map/ts,rsp->rtp/dot_general | solution.py:58
  118.0 45.7 %all-to-all-done.1 = f32[128,16,384]{2,1,0:T(8,128)} async-done(((f32[128,16,384]{2,1,0:T(8,128)}), f32[128,16,384]{2,1,0:T(8,128)}, u32[]{:S(2)}, u32[]{:S(2)}) %all-to-all-start.1) | async-done | bytes 3145760 | tf_op jit(solution)/shard_map/all_to_all | solution.py:57
  163.8 2.3 copy.28
  166.6 1.0 copy-done.6
  167.5 9.9 %fusion.5 = f32[1,8,256,384]{3,2,1,0:T(8,128)S(1)} fusion(f32[8,384,256]{1,2,0:T(8,128)} %fusion.24, f32[8,16,16,384]{3,2,1,0:T(8,128)S(1)} %copy.28, f32[1,8,256,384]{3,2,1,0:T(8,128)} %param.9, f32[1,8,256,384]{3,2,1,0:T(8,128)} %collective-permute-done.1, f32[1,8,256,384]{3,2,1,0:T(8,128)} %collective-permute-done, f32[8,256,384]{2,1,0:T(8,128)S(1)} %copy-done.6, ...), kind=kOutput, calls=%fused_computation.9 | convolution fusion | flops 3634888704 | bytes 25763912 | tf_op jit(solution)/shard_map/dot_general | solution.py:60
  177.8 1.3 copy-done.4
  179.1 84.5 %all_to_all.47 = f32[16,8,16,384]{3,2,1,0:T(8,128)S(1)} all-to-all(f32[16,8,16,384]{3,2,1,0:T(8,128)S(1)} %fusion.26), channel_id=1, replica_groups=mesh['ka'=2,'slab'=16] {'slab'}, dimensions={0} | all-to-all | bytes 6291456 | tf_op jit(solution)/shard_map/all_to_all | solution.py:20
  263.6 7.1 %fusion.17 = f32[128,16,384]{0,2,1:T(8,128)} fusion(f32[128,16,384]{2,1,0:T(8,128)S(1)} %bitcast.250, f32[128,128]{1,0:T(8,128)S(1)} %copy-done.8), kind=kOutput, calls=%fused_computation.23 | convolution fusion | flops 1207959552 | bytes 6356992 | tf_op jit(solution)/shard_map/sr,rtp->stp/dot_general | solution.py:45
  270.7 3.7 copy.30
  274.4 4.5 %all-to-all-start.3 = ((f32[128,16,384]{2,1,0:T(8,128)}), f32[128,16,384]{2,1,0:T(8,128)}, u32[]{:S(2)}, u32[]{:S(2)}) async-start(f32[128,16,384]{2,1,0:T(8,128)} %copy.30), calls=%async_computation.3 | async-start | bytes 6291456 | tf_op jit(solution)/shard_map/all_to_all | solution.py:57
  278.9 1.3 collective-permute-start.2
  280.2 6.3 %collective-permute-start.3 = (f32[1,8,256,384]{3,2,1,0:T(8,128)}, f32[1,8,256,384]{3,2,1,0:T(8,128)}, u32[]{:S(2)}, u32[]{:S(2)}) collective-permute-start(f32[1,8,256,384]{3,2,1,0:T(8,128)} %copy-done.4), channel_id=1, source_target_pairs={{0,16},{1,17},{2,18},{3,19},{4,20},{5,21},{6,22},{7,23},{8,24},{9,... | collective-permute-start | bytes 9437192 | tf_op jit(solution)/shard_map/ppermute | solution.py:35
  286.6 6.5 %fusion.22 = f32[8,384,256]{1,2,0:T(8,128)} fusion(f32[256,256]{1,0:T(8,128)S(1)} %copy-done.7, f32[1,8,256,384]{3,2,1,0:T(8,128)} %copy-done.4), kind=kOutput, calls=%fused_computation.26 | convolution fusion | flops 2415919104 | bytes 6553600 | tf_op jit(solution)/shard_map/ts,rsp->rtp/dot_general | solution.py:58
  293.1 46.0 %all-to-all-done.3 = f32[128,16,384]{2,1,0:T(8,128)} async-done(((f32[128,16,384]{2,1,0:T(8,128)}), f32[128,16,384]{2,1,0:T(8,128)}, u32[]{:S(2)}, u32[]{:S(2)}) %all-to-all-start.3) | async-done | bytes 3145760 | tf_op jit(solution)/shard_map/all_to_all | solution.py:57
  339.0 2.3 copy.31
  341.9 1.0 copy-done.5
  342.8 12.1 %multiply_reduce_fusion.1 = (f32[]{:T(128)}, f32[]{:T(128)}, f32[1,8,256,384]{3,2,1,0:T(8,128)}) fusion(f32[1,8,256,384]{3,2,1,0:T(8,128)S(1)} %copy-done.3, f32[1,8,256,384]{3,2,1,0:T(8,128)S(1)} %copy-done.5, f32[1,8,256,384]{3,2,1,0:T(8,128)} %collective-permute-done.3, f32[]{:T(128)S(6)} %div.20, f32[1,8,256,384]{3,2,1,0:T(8,128)} %collective-permute-done.2, ...), kind=kOutput, calls=%fused_computation.21 | convolution fusion | flops 3638034432 | bytes 25763920 | tf_op jit(solution)/shard_map/dot_general | solution.py:60
  355.0 49.6 %all-reduce = (f32[1]{0:T(128)}, f32[1]{0:T(128)}) all-reduce(f32[1]{0:T(128)} %bitcast.55, f32[1]{0:T(128)} %bitcast.53), channel_id=1, replica_groups=mesh['ka'=2,'slab'=16] {'slab'}, use_global_device_ids=true, to_apply=%region_3.0 | all-reduce | flops 2 | bytes 16 | tf_op jit(solution)/shard_map/psum | solution.py:81
  (52 shorter events, 2.0 us)
Async XLA Ops:
  0.6 165.5 %copy-start = (f32[384,384]{1,0:T(8,128)S(1)}, f32[384,384]{1,0:T(8,128)}, u32[]{:S(2)}) copy-start(f32[384,384]{1,0:T(8,128)} %param.14) | copy-start | bytes 1769476
  0.6 7.8 %copy-start.1 = (f32[1,8,256,384]{3,2,1,0:T(8,128)S(1)}, f32[1,8,256,384]{3,2,1,0:T(8,128)}, u32[]{:S(2)}) copy-start(f32[1,8,256,384]{3,2,1,0:T(8,128)} %param.10) | copy-start | bytes 9437188
  8.7 79.6 %copy-start.8 = (f32[128,128]{1,0:T(8,128)S(1)}, f32[128,128]{1,0:T(8,128)}, u32[]{:S(2)}) copy-start(f32[128,128]{1,0:T(8,128)} %param.12) | copy-start | bytes 196612
  98.9 12.5 %copy-start.11 = (f32[8]{0:T(128)S(1)}, f32[8]{0:T(128)}, u32[]{:S(2)}) copy-start(f32[8]{0:T(128)} %param.16) | copy-start | bytes 100
  98.9 12.5 %copy-start.10 = (f32[256]{0:T(256)S(1)}, f32[256]{0:T(256)}, u32[]{:S(2)}) copy-start(f32[256]{0:T(256)} %param.17) | copy-start | bytes 3076
  98.9 12.6 %copy-start.7 = (f32[256,256]{1,0:T(8,128)S(1)}, f32[256,256]{1,0:T(8,128)}, u32[]{:S(2)}) copy-start(f32[256,256]{1,0:T(8,128)} %param.13) | copy-start | bytes 786436
  98.9 64.8 %all-to-all-start.1 = ((f32[128,16,384]{2,1,0:T(8,128)}), f32[128,16,384]{2,1,0:T(8,128)}, u32[]{:S(2)}, u32[]{:S(2)}) async-start(f32[128,16,384]{2,1,0:T(8,128)} %copy.27), calls=%async_computation.1 | async-start | bytes 6291456 | tf_op jit(solution)/shard_map/all_to_all | solution.py:57
  103.6 62.5 %collective-permute-start = (f32[1,8,256,384]{3,2,1,0:T(8,128)}, f32[1,8,256,384]{3,2,1,0:T(8,128)}, u32[]{:S(2)}, u32[]{:S(2)}) collective-permute-start(f32[1,8,256,384]{3,2,1,0:T(8,128)} %param.10), channel_id=1, source_target_pairs={{16,0},{17,1},{18,2},{19,3},{20,4},{21,5},{22,6},{23,7},{24,8},{25... | collective-permute-start | bytes 9437192 | tf_op jit(solution)/shard_map/ppermute | solution.py:37
  104.9 61.2 %collective-permute-start.1 = (f32[1,8,256,384]{3,2,1,0:T(8,128)}, f32[1,8,256,384]{3,2,1,0:T(8,128)}, u32[]{:S(2)}, u32[]{:S(2)}) collective-permute-start(f32[1,8,256,384]{3,2,1,0:T(8,128)} %param.10), channel_id=1, source_target_pairs={{0,16},{1,17},{2,18},{3,19},{4,20},{5,21},{6,22},{7,23},{8,24},{9,... | collective-permute-start | bytes 9437192 | tf_op jit(solution)/shard_map/ppermute | solution.py:35
  111.5 54.6 %copy-start.9 = (f32[8]{0:T(128)S(1)}, f32[8]{0:T(128)}, u32[]{:S(2)}) copy-start(f32[8]{0:T(128)} %param.15) | copy-start | bytes 100
  163.7 2.8 copy-start.2
  163.8 3.8 copy-start.6
  177.4 1.7 copy-start.4
  274.4 64.6 %all-to-all-start.3 = ((f32[128,16,384]{2,1,0:T(8,128)}), f32[128,16,384]{2,1,0:T(8,128)}, u32[]{:S(2)}, u32[]{:S(2)}) async-start(f32[128,16,384]{2,1,0:T(8,128)} %copy.30), calls=%async_computation.3 | async-start | bytes 6291456 | tf_op jit(solution)/shard_map/all_to_all | solution.py:57
  278.9 62.5 %collective-permute-start.2 = (f32[1,8,256,384]{3,2,1,0:T(8,128)}, f32[1,8,256,384]{3,2,1,0:T(8,128)}, u32[]{:S(2)}, u32[]{:S(2)}) collective-permute-start(f32[1,8,256,384]{3,2,1,0:T(8,128)} %copy-done.4), channel_id=1, source_target_pairs={{16,0},{17,1},{18,2},{19,3},{20,4},{21,5},{22,6},{23,7},{24,8},{25... | collective-permute-start | bytes 9437192 | tf_op jit(solution)/shard_map/ppermute | solution.py:37
  280.2 61.2 %collective-permute-start.3 = (f32[1,8,256,384]{3,2,1,0:T(8,128)}, f32[1,8,256,384]{3,2,1,0:T(8,128)}, u32[]{:S(2)}, u32[]{:S(2)}) collective-permute-start(f32[1,8,256,384]{3,2,1,0:T(8,128)} %copy-done.4), channel_id=1, source_target_pairs={{0,16},{1,17},{2,18},{3,19},{4,20},{5,21},{6,22},{7,23},{8,24},{9,... | collective-permute-start | bytes 9437192 | tf_op jit(solution)/shard_map/ppermute | solution.py:35
  339.0 2.8 copy-start.3
  339.0 3.8 copy-start.5
